TPU v7x, 512 devices: a whole 4x8x8 slice. The times are simulated.
512 devices in a mesh: dp: 128 (over z_hi, y, x), feat: 4 (over z_lo, core).
Axes of the slice: x: 4, y: 8, z: 8 (z_hi: 4, z_lo: 2; z = z_hi * 2 + z_lo), core: 2. Of those that a mesh axis runs over, the one named last changes fastest.
Arguments:
- train_grads: bfloat16 [131072, 4096], P('dp', 'feat')
- token_counts: int32 [131072], P('dp'), may hold values from 1 to 1024, as said below
- train_ids: int32 [131072], P('dp'), may hold values from 0 to 49151
- query_grads: bfloat16 [24576, 4096], P('dp', 'feat')
- query_ids: int32 [24576], P('dp'), may hold values from 0 to 49151
Outputs:
- influence: float32 [4, 192, 131072], P(None, 'feat', 'dp')
Inputs may be any that keep to these rules, and one draw needn't show every extreme that they name: `token_counts`: some training example has exactly 1024 tokens and some exactly one.
All inputs are finite; a program needn't handle non-finite values.
Results may differ from a plain program's by a relative error of at most 0.00115.
The roundings to bfloat16 on the way count: a program that leaves them out, or rounds other values in their place, can miss the bound.
Values may be sent and summed in bfloat16 or wider, within the bound.
A program may use at most 64 MiB of HBM per device.

v0:
```python
import jax
import jax.numpy as jnp
from jax import lax
from jax.sharding import PartitionSpec as P

KOUT = 64
KIN = 64
STEPS = 4


damping = 0.1


def passed_along(block, axis, distance):
    devices = range(lax.axis_size(axis))
    route = [((i - distance) % len(devices), i) for i in devices]
    return lax.ppermute(block, axis, route)


def inverse(matrix):
    factor = jnp.linalg.cholesky(matrix)
    return jax.scipy.linalg.cho_solve((factor, True), jnp.eye(matrix.shape[0], dtype=matrix.dtype))


def folder(left_rows, width):

    def accumulate(folded, portion, offset):
        rows_in = portion.shape[1] // width
        first_row = offset // width
        columns = lax.dynamic_slice_in_dim(left_rows, first_row, rows_in, 1)
        pieces = portion.astype(jnp.float32).reshape(portion.shape[0], rows_in, width)
        return folded + jnp.einsum("ac,qcb->qab", columns, pieces, precision=lax.Precision.HIGHEST)

    return accumulate


def finish(folded, right_inv, mean_total):
    mixed_rows = (
        jnp.einsum("qab,bd->qad", folded, right_inv, precision=lax.Precision.HIGHEST) * mean_total
    )
    return mixed_rows.reshape(folded.shape[0], -1).astype(jnp.bfloat16)


def on_device(train_grads, token_counts, train_ids, query_grads, query_ids):
    feat_count = lax.axis_size("feat")
    feat_index = lax.axis_index("feat")
    ex_rows = train_grads.shape[0]
    quarter = ex_rows // feat_count
    total_rows = ex_rows * lax.axis_size("dp")
    features = (train_grads.astype(jnp.float32) / token_counts[:, None].astype(jnp.float32)).astype(
        jnp.bfloat16
    )
    regrouped = lax.all_to_all(features, "feat", split_axis=0, concat_axis=1, tiled=True)
    matrices = regrouped.reshape(quarter, KOUT, KIN)
    right_part = jnp.einsum("eab,eac->bc", matrices, matrices, preferred_element_type=jnp.float32)
    left_part = jnp.einsum("eab,ecb->ac", matrices, matrices, preferred_element_type=jnp.float32)
    right_factor, left_factor = lax.psum((right_part, left_part), ("dp", "feat"))
    mean_total = jnp.trace(right_factor) / total_rows
    right_inv = inverse(
        right_factor / total_rows + damping * mean_total / KIN * jnp.eye(KIN, dtype=jnp.float32)
    )
    left_inv = inverse(
        left_factor / total_rows + damping * mean_total / KOUT * jnp.eye(KOUT, dtype=jnp.float32)
    )
    left_rows = lax.dynamic_slice_in_dim(
        left_inv, feat_index * (KOUT // feat_count), KOUT // feat_count, 0
    )
    accumulate = folder(left_rows, KIN)
    start_fold = jnp.zeros((query_grads.shape[0], left_rows.shape[0], KIN), jnp.float32)
    folded = accumulate(
        start_fold, lax.all_gather(query_grads, "feat", axis=1, tiled=True), jnp.int32(0)
    )
    anchor = (finish(folded, right_inv, mean_total), query_ids)
    arrivals = [anchor]
    current = anchor
    for shift_step in range(1, STEPS):
        current = passed_along((current[0], current[1]), "dp", 1)
        arrivals.append(current)
    score_tiles = []
    for query_block, block_ids in arrivals:
        score_tile = lax.dot_general(
            query_block, features, (((1,), (1,)), ((), ())), preferred_element_type=jnp.float32
        )
        score_tile = jnp.where(
            block_ids[:, None] == train_ids[None, :], jnp.zeros_like(score_tile), score_tile
        )
        score_tiles.append(lax.psum_scatter(score_tile, "feat", scatter_dimension=0, tiled=True))
    stacked = jnp.stack(score_tiles, 0)
    return stacked


def solution(mesh):
    in_specs = (P("dp", "feat"), P("dp"), P("dp"), P("dp", "feat"), P("dp"))
    out_specs = P(None, "feat", "dp")
    return jax.shard_map(
        on_device, mesh=mesh, in_specs=in_specs, out_specs=out_specs, check_vma=False
    )
```

profile of v0, /device:TPU:1, one launch (start us, length us, event | category | flops | bytes accessed | tf_op | source)
XLA Modules:
  0.0 377.1 jit_solution(16762052486272689972)
XLA Ops:
  6.5 0.7 convert_element_type.26
  7.2 3.7 divide_convert_fusion
  11.0 10.6 %all-to-all-start = ((bf16[4,256,1024]{2,1,0:T(8,128)(2,1)}), bf16[4,256,1024]{2,1,0:T(8,128)(2,1)S(1)}, u32[]{:S(2)}, u32[]{:S(2)}) async-start(bf16[4,256,1024]{2,1,0:T(8,128)(2,1)} %bitcast), calls=%async_computation | async-start | bytes 4194304 | tf_op jit(solution)/shard_map/all_to_all | solution.py:53
  21.6 1.0 copy.25
  22.6 28.2 %all-to-all-done = bf16[4,256,1024]{2,1,0:T(8,128)(2,1)S(1)} async-done(((bf16[4,256,1024]{2,1,0:T(8,128)(2,1)}), bf16[4,256,1024]{2,1,0:T(8,128)(2,1)S(1)}, u32[]{:S(2)}, u32[]{:S(2)}) %all-to-all-start) | async-done | bytes 2097184 | tf_op jit(solution)/shard_map/all_to_all | solution.py:53
  50.9 1.3 copy-done
  52.2 2.8 copy.19
  55.1 0.7 convolution_bitcast_fusion.1
  55.7 3.3 fusion.8
  59.1 99.8 %all-reduce = (f32[64,64]{0,1:T(8,128)S(1)}, f32[64,64]{0,1:T(8,128)S(1)}) all-reduce(f32[64,64]{0,1:T(8,128)S(1)} %convolution_bitcast_fusion.1, f32[64,64]{0,1:T(8,128)S(1)} %fusion.8), channel_id=1, replica_groups=mesh['dp'=128,'feat'=4] {'dp','feat'}, use_global_device_ids=true, to_apply=%region_1.0 | all-reduce | flops 8192 | bytes 65536 | tf_op jit(solution)/shard_map/psum | solution.py:57
  158.9 0.6 select_reduce_fusion.2
  160.1 0.1 copy.24
  160.2 5.8 %cholesky.44 = f32[64,64]{1,0:T(8,128)S(1)} custom-call(f32[64,64]{1,0:T(8,128)S(1)} %fusion.24), custom_call_target="Cholesky" | custom-call | tf_op jit(solution)/shard_map/jit(cholesky)/cholesky | solution.py:21
  166.1 0.7 compare_reduce_fusion.1
  166.8 0.7 fusion.16
  167.5 4.9 %custom-call.8 = f32[1,64,64]{1,2,0:T(8,128)S(1)} custom-call(f32[1,64,64]{2,1,0:T(8,128)S(1)} %fusion.16), custom_call_target="InvertDiagBlocksLowerTriangular" | custom-call | tf_op jit(solution)/shard_map/jit(_cho_solve)/triangular_solve | solution.py:22
  172.4 0.1 copy.27
  172.5 5.8 %cholesky.55 = f32[64,64]{1,0:T(8,128)S(1)} custom-call(f32[64,64]{1,0:T(8,128)S(1)} %fusion.20), custom_call_target="Cholesky" | custom-call | tf_op jit(solution)/shard_map/jit(cholesky)/cholesky | solution.py:21
  178.4 0.7 compare_reduce_fusion
  179.2 0.7 fusion.17
  179.9 4.9 %custom-call.9 = f32[1,64,64]{1,2,0:T(8,128)S(1)} custom-call(f32[1,64,64]{2,1,0:T(8,128)S(1)} %fusion.17), custom_call_target="InvertDiagBlocksLowerTriangular" | custom-call | tf_op jit(solution)/shard_map/jit(_cho_solve)/triangular_solve | solution.py:22
  185.4 0.2 fusion.12
  185.6 0.2 convolution_bitcast_fusion
  185.9 0.2 fusion.14
  186.1 0.2 fusion.21
  186.3 3.4 fusion.4
  189.7 1.7 fusion.7
  191.5 2.4 collective-permute-start.1
  193.9 3.4 convolution_select_fusion
  197.4 25.1 %collective-permute-done.1 = bf16[192,1024]{0,1:T(8,128)(2,1)S(1)} collective-permute-done((bf16[192,1024]{0,1:T(8,128)(2,1)S(1)}, bf16[192,1024]{0,1:T(8,128)(2,1)S(1)}, u32[]{:S(2)}, u32[]{:S(2)}) %collective-permute-start.1) | collective-permute-done | bytes 393248 | tf_op jit(solution)/shard_map/ppermute | solution.py:17
  222.5 1.9 collective-permute-start.3
  224.4 1.9 collective-permute-start
  226.3 24.9 %collective-permute-done = s32[192]{0:T(256)S(1)} collective-permute-done((s32[192]{0:T(256)S(1)}, s32[192]{0:T(256)S(1)}, u32[]{:S(2)}, u32[]{:S(2)}) %collective-permute-start) | collective-permute-done | bytes 800 | tf_op jit(solution)/shard_map/ppermute | solution.py:17
  251.2 1.9 collective-permute-start.2
  253.1 8.7 %collective-permute-done.2 = s32[192]{0:T(256)S(1)} collective-permute-done((s32[192]{0:T(256)S(1)}, s32[192]{0:T(256)S(1)}, u32[]{:S(2)}, u32[]{:S(2)}) %collective-permute-start.2) | collective-permute-done | bytes 800 | tf_op jit(solution)/shard_map/ppermute | solution.py:17
  261.8 1.9 collective-permute-start.4
  263.8 1.9 collective-permute-start.5
  265.7 2.4 fusion.28
  268.1 2.5 fusion.29
  270.6 1.9 collective-permute-done.4
  272.5 15.5 %collective-permute-done.5 = bf16[192,1024]{0,1:T(8,128)(2,1)S(1)} collective-permute-done((bf16[192,1024]{0,1:T(8,128)(2,1)S(1)}, bf16[192,1024]{0,1:T(8,128)(2,1)S(1)}, u32[]{:S(2)}, u32[]{:S(2)}) %collective-permute-start.5) | collective-permute-done | bytes 393248 | tf_op jit(solution)/shard_map/ppermute | solution.py:17
  288.0 3.9 %compare_select_fusion.2 = (f32[192,1024]{1,0:T(8,128)}, f32[192,1024]{1,0:T(8,128)}, f32[192,1024]{1,0:T(8,128)}) fusion(f32[192,1024]{1,0:T(8,128)S(1)} %fusion.28, s32[1024]{0:T(1024)S(1)} %copy-done.2, s32[192]{0:T(256)S(1)} %collective-permute-done, f32[192,1024]{1,0:T(8,128)S(1)} %fusion.29, s32[192]{0:T(256)S(1)} %collective-permute-done.2, ...), kind=kOutput, calls=%fused_computation.16 | convolution fusion | flops 403832832 | bytes 6428928 | tf_op jit(solution)/shard_map/dot_general | solution.py:81
  292.0 0.5 reduce-scatter.9.cloned.1.call-update
  292.6 0.5 reduce-scatter.11.cloned.1.call-update
  293.2 19.7 %reduce-scatter.7.cloned.1.call-done = f32[48,1024]{1,0:T(8,128)} async-done(((f32[192,1024]{1,0:T(8,128)}), f32[48,1024]{1,0:T(8,128)}) %reduce-scatter.7.cloned.1.call-update) | async-done | bytes 196624 | tf_op jit(solution)/shard_map/reduce_scatter | solution.py:87
  312.9 27.8 %reduce-scatter.9.cloned.1.call-done = f32[48,1024]{1,0:T(8,128)} async-done(((f32[192,1024]{1,0:T(8,128)}), f32[48,1024]{1,0:T(8,128)}) %reduce-scatter.9.cloned.1.call-update) | async-done | bytes 196624 | tf_op jit(solution)/shard_map/reduce_scatter | solution.py:87
  340.7 27.7 %reduce-scatter.11.cloned.1.call-done = f32[48,1024]{1,0:T(8,128)} async-done(((f32[192,1024]{1,0:T(8,128)}), f32[48,1024]{1,0:T(8,128)}) %reduce-scatter.11.cloned.1.call-update) | async-done | bytes 196624 | tf_op jit(solution)/shard_map/reduce_scatter | solution.py:87
  368.4 2.2 pad_maximum_fusion
  (23 shorter events, 0.4 us)
Async XLA Ops:
  11.0 10.6 %copy-start.1 = (bf16[192,1024]{1,0:T(8,128)(2,1)S(1)}, bf16[192,1024]{1,0:T(8,128)(2,1)}, u32[]{:S(2)}) copy-start(bf16[192,1024]{1,0:T(8,128)(2,1)} %param.11) | copy-start | bytes 1179652
  11.0 39.9 %all-to-all-start = ((bf16[4,256,1024]{2,1,0:T(8,128)(2,1)}), bf16[4,256,1024]{2,1,0:T(8,128)(2,1)S(1)}, u32[]{:S(2)}, u32[]{:S(2)}) async-start(bf16[4,256,1024]{2,1,0:T(8,128)(2,1)} %bitcast), calls=%async_computation | async-start | bytes 4194304 | tf_op jit(solution)/shard_map/all_to_all | solution.py:53
  21.6 164.7 %all-gather.2.cloned.1.call-start = ((), (), s32[]{:S(2)}) async-start(), calls=%async_computation.5 | async-start | bytes 2621440 | tf_op jit(solution)/shard_map/all_gather | solution.py:71
  22.6 270.6 %reduce-scatter.5.cloned.1.call-start = ((), (), s32[]{:S(2)}) async-start(), calls=%async_computation.6 | async-start | bytes 983040 | tf_op jit(solution)/shard_map/reduce_scatter | solution.py:87
  50.9 1.3 copy-start
  186.3 7.6 %copy-start.2 = (s32[1024]{0:T(1024)S(1)}, s32[1024]{0:T(1024)}, u32[]{:S(2)}) copy-start(s32[1024]{0:T(1024)} %param.10) | copy-start | bytes 12292
  186.3 7.6 %copy-start.3 = (s32[192]{0:T(256)S(1)}, s32[192]{0:T(256)}, u32[]{:S(2)}) copy-start(s32[192]{0:T(256)} %param.12) | copy-start | bytes 2308
  191.5 31.0 %collective-permute-start.1 = (bf16[192,1024]{0,1:T(8,128)(2,1)S(1)}, bf16[192,1024]{0,1:T(8,128)(2,1)S(1)}, u32[]{:S(2)}, u32[]{:S(2)}) collective-permute-start(bf16[192,1024]{0,1:T(8,128)(2,1)S(1)} %bitcast.58), channel_id=1, source_target_pairs={{508,0},{0,4},{4,8},{8,12},{12,16},{16,20},{20,24},{24,28},{28,32}... | collective-permute-start | bytes 1179656 | tf_op jit(solution)/shard_map/ppermute | solution.py:17
  197.3 115.5 %reduce-scatter.7.cloned.1.call-start = ((), (), s32[]{:S(2)}) async-start(), calls=%async_computation.7 | async-start | bytes 983040 | tf_op jit(solution)/shard_map/reduce_scatter | solution.py:87
  222.5 41.3 %collective-permute-start.3 = (bf16[192,1024]{0,1:T(8,128)(2,1)S(1)}, bf16[192,1024]{0,1:T(8,128)(2,1)S(1)}, u32[]{:S(2)}, u32[]{:S(2)}) collective-permute-start(bf16[192,1024]{0,1:T(8,128)(2,1)S(1)} %collective-permute-done.1), channel_id=1, source_target_pairs={{508,0},{0,4},{4,8},{8,12},{12,16},{16,20},{20,24},{24,28},{28,32}... | collective-permute-start | bytes 1179656 | tf_op jit(solution)/shard_map/ppermute | solution.py:17
  224.4 26.8 %collective-permute-start = (s32[192]{0:T(256)S(1)}, s32[192]{0:T(256)S(1)}, u32[]{:S(2)}, u32[]{:S(2)}) collective-permute-start(s32[192]{0:T(256)S(1)} %copy-done.3), channel_id=1, source_target_pairs={{508,0},{0,4},{4,8},{8,12},{12,16},{16,20},{20,24},{24,28},{28,32}... | collective-permute-start | bytes 2312 | tf_op jit(solution)/shard_map/ppermute | solution.py:17
  251.2 10.6 %collective-permute-start.2 = (s32[192]{0:T(256)S(1)}, s32[192]{0:T(256)S(1)}, u32[]{:S(2)}, u32[]{:S(2)}) collective-permute-start(s32[192]{0:T(256)S(1)} %collective-permute-done), channel_id=1, source_target_pairs={{508,0},{0,4},{4,8},{8,12},{12,16},{16,20},{20,24},{24,28},{28,32}... | collective-permute-start | bytes 2312 | tf_op jit(solution)/shard_map/ppermute | solution.py:17
  261.8 10.6 %collective-permute-start.4 = (s32[192]{0:T(256)S(1)}, s32[192]{0:T(256)S(1)}, u32[]{:S(2)}, u32[]{:S(2)}) collective-permute-start(s32[192]{0:T(256)S(1)} %collective-permute-done.2), channel_id=1, source_target_pairs={{508,0},{0,4},{4,8},{8,12},{12,16},{16,20},{20,24},{24,28},{28,32}... | collective-permute-start | bytes 2312 | tf_op jit(solution)/shard_map/ppermute | solution.py:17
  263.8 24.2 %collective-permute-start.5 = (bf16[192,1024]{0,1:T(8,128)(2,1)S(1)}, bf16[192,1024]{0,1:T(8,128)(2,1)S(1)}, u32[]{:S(2)}, u32[]{:S(2)}) collective-permute-start(bf16[192,1024]{0,1:T(8,128)(2,1)S(1)} %collective-permute-done.3), channel_id=1, source_target_pairs={{508,0},{0,4},{4,8},{8,12},{12,16},{16,20},{20,24},{24,28},{28,32}... | collective-permute-start | bytes 1179656 | tf_op jit(solution)/shard_map/ppermute | solution.py:17
  292.0 48.7 %reduce-scatter.9.cloned.1.call-start = ((), (), s32[]{:S(2)}) async-start(), calls=%async_computation.8 | async-start | bytes 983040 | tf_op jit(solution)/shard_map/reduce_scatter | solution.py:87
  292.5 75.8 %reduce-scatter.11.cloned.1.call-start = ((), (), s32[]{:S(2)}) async-start(), calls=%async_computation.9 | async-start | bytes 983040 | tf_op jit(solution)/shard_map/reduce_scatter | solution.py:87
Sparse Core Ops, SparseCore 0:
  24.5 39.4 all-gather.1
  197.5 20.8 reduce-scatter.4
  292.1 20.7 reduce-scatter.6
  315.6 25.0 reduce-scatter.8
  343.4 24.9 reduce-scatter.10
where the time goes:
time: 378 us; the launch traced here: 377 us
  waiting for transfers between devices  181 us (48%)
  blocking collectives  99.8 us (26%)
  other arithmetic  31.7 us (8%)
  starting transfers between devices  22.8 us (6%)
  matrix products  22.2 us (6%)
  between operations  14.6 us (4%)
  local copies, waits for them, and re-layouts  5.35 us (1%)
    psum x1, blocking collectives, on_device(): lax.psum((right_part, left_part), ('dp', 'feat'))  99.8 us
    ppermute x6, waiting for transfers between devices, passed_along(): return lax.ppermute(block, axis, route)  76.1 us
    reduce_scatter x4, waiting for transfers between devices, on_device(): lax.psum_scatter(score_tile, 'feat', scatter_dimension=0, tiled=True)  75.2 us
    all_to_all x1, waiting for transfers between devices, on_device(): lax.all_to_all(features, 'feat', split_axis=0, concat_axis=1, tiled=True)  28.2 us
    another operation x6, other arithmetic, inverse(): factor = jnp.linalg.cholesky(matrix)  13.2 us
    dot_general x4, matrix products, on_device(): lax.dot_general(query_block, features, (((1,), (1,)), ((), ())), preferre...  12.2 us
    ppermute x6, starting transfers between devices, passed_along(): return lax.ppermute(block, axis, route)  12 us
    another operation x4, other arithmetic, inverse(): jax.scipy.linalg.cho_solve((factor, True), jnp.eye(matrix.shape[0], dtype...  11.2 us
  transfers between devices with their start and end apart: 12, of which 9 were waited for; matrix products, arithmetic and copies ran while one was open for 12% of the time, Pallas kernels for 0%

commit v1 on v0

v1 whole, which is shorter than its diff:
```python
import jax
import jax.numpy as jnp
from jax import lax
from jax.experimental import pallas as pl
from jax.experimental.pallas import tpu as pltpu
from jax.sharding import PartitionSpec as P

K = 64
STEPS = 4
NX, NY, NZ, NF = 4, 8, 4, 4
N_DP = NX * NY * NZ
TRAIN = 131072
EX = 1024
COLS = 1024
PART = EX // NF
HALF = PART // 2
QD = 192
QROWS = QD // NF
DAMPING = 0.1

F32 = jnp.float32
BF16 = jnp.bfloat16


def dot_nt(a, b):
    return lax.dot_general(a, b, (((1,), (1,)), ((), ())), preferred_element_type=F32)


def dot_nn(a, b):
    return lax.dot_general(a, b, (((1,), (0,)), ((), ())), preferred_element_type=F32)


def identity(n):
    rows = lax.broadcasted_iota(jnp.int32, (n, n), 0)
    cols = lax.broadcasted_iota(jnp.int32, (n, n), 1)
    return jnp.where(rows == cols, 1.0, 0.0).astype(BF16)


def lower_lanes(rows):
    return lax.broadcasted_iota(jnp.int32, (rows, 2 * K), 1) < K


def fold(g):
    low = lower_lanes(K)
    h = jnp.where(low, g[0:64, 0:128], g[64:128, 0:128]) + jnp.where(
        low, g[128:192, 128:256], g[192:256, 128:256]
    )
    both = h + pltpu.roll(h, K, 1)
    return jnp.where(lower_lanes(32), both[0:32], both[32:64])


def split(v):
    high = v.astype(BF16)
    return high, (v - high.astype(F32)).astype(BF16)


def kernel(
    tg, qg, cnt, tid, qid, out,
    xr, xto, xt, xb, xbt, qall, prev, ids, prev_ids, m, w, st, acc, tcol,
    packed, rs_in, part, x_in, y_in, z_in, total, whole, inv, rsm, lsm,
    send, recv, local_sem,
):
    f = lax.axis_index("feat")
    i = lax.axis_index("dp")
    x = i % NX
    y = (i // NX) % NY
    zh = i // (NX * NY)

    def mate(d):
        if d == 0:
            return f
        if d == 1:
            return f + 1 - 2 * (f % 2)
        if d == 2:
            return (f + 2) % 4
        return 3 - f

    def on_x(d):
        return i - x + (x + d) % NX

    def on_y(d):
        return (zh * NY + (y + d) % NY) * NX + x

    def on_z(d):
        return (((zh + d) % NZ) * NY + y) * NX + x

    used = [0]

    def copy(src, dst, dp, ft, at=None):
        if at is None:
            at = used[0]
            used[0] += 1
        return pltpu.make_async_remote_copy(
            src_ref=src, dst_ref=dst, send_sem=send.at[at], recv_sem=recv.at[at],
            device_id=(dp, ft), device_id_type=pl.DeviceIdType.MESH,
        )

    barrier = pltpu.get_barrier_semaphore()
    partners = [(i, mate(d)) for d in (1, 2, 3)]
    partners += [(on_x(d), f) for d in range(1, NX)]
    partners += [(on_y(d), f) for d in range(1, NY)]
    partners += [(on_z(d), f) for d in range(1, NZ)]
    partners += [((i + NX) % N_DP, f), ((i + N_DP - NX) % N_DP, f)]
    for dp, ft in partners:
        pl.semaphore_signal(barrier, inc=1, device_id=(dp, ft), device_id_type=pl.DeviceIdType.MESH)
    pl.semaphore_wait(barrier, len(partners))

    sent = []

    def go(c):
        c.start()
        sent.append(c)
        return c

    regroup = {}
    for half in range(2):
        for d in (2, 3):
            rows = pl.ds(pl.multiple_of(mate(d) * PART + half * HALF, HALF), HALF)
            regroup[half, d] = go(copy(
                tg.at[rows, :], xr.at[d - 1, pl.ds(half * HALF, HALF), :], i, mate(d)))
    for half in range(2):
        rows = pl.ds(pl.multiple_of(mate(1) * PART + half * HALF, HALF), HALF)
        regroup[half, 1] = go(copy(
            tg.at[rows, :], xr.at[0, pl.ds(half * HALF, HALF), :], i, mate(1)))

    ids[0] = jnp.broadcast_to(qid[...], (8, 256))
    next_row = (i + NX) % N_DP
    to_prev = go(copy(qg, prev, next_row, f))
    to_prev_ids = go(copy(ids.at[0], prev_ids, next_row, f))
    right, left = on_x(1), on_x(NX - 1)

    def along(slot, src, src_ids, dp, at):
        return (copy(src, qall.at[slot, 0], dp, f, at), copy(src_ids, ids.at[slot], dp, f, at + 1))

    at_right = used[0]
    at_left = used[0] + 2
    at_relay_r = used[0] + 4
    at_relay_l = used[0] + 6
    used[0] += 8
    own_right = along(1, qg, ids.at[0], right, at_right)
    prev_right = along(1, prev, prev_ids, right, at_right)
    own_left = along(3, qg, ids.at[0], left, at_left)
    prev_left = along(3, prev, prev_ids, left, at_left)

    @pl.when(x < NX - 1)
    def _():
        for c in own_right:
            c.start()

    @pl.when(x == 0)
    def _():
        for c in own_left:
            c.start()

    core_a = [None] * STEPS
    z_a = [None] * STEPS
    core_b = [None] * STEPS
    for s in range(STEPS):
        src = qg if s == 0 else qall.at[s, 0]
        core_a[s] = copy(src, qall.at[s, 1], i, mate(1))
        z_a[s] = copy(src, qall.at[s, 2], i, mate(2))
        core_b[s] = copy(qall.at[s, 2], qall.at[s, 3], i, mate(1))
    go(core_a[0])

    qall[0, 0] = qg[...]

    def stages(n):
        c = {}
        c["rs"] = [copy(packed.at[n, pl.ds(pl.multiple_of(mate(d) * 8, 8), 8), :],
                        rs_in.at[n, d - 1], i, mate(d)) for d in (1, 2, 3)]
        c["x"] = [copy(part.at[n, 0], x_in.at[n, d - 1], on_x(d), f) for d in range(1, NX)]
        c["y"] = [copy(part.at[n, 1], y_in.at[n, d - 1], on_y(d), f) for d in range(1, NY)]
        c["z"] = [copy(part.at[n, 2], z_in.at[n, d - 1], on_z(d), f) for d in range(1, NZ)]
        c["ag"] = [copy(total.at[n, 0], total.at[n, d], i, mate(d)) for d in (1, 2, 3)]
        return c

    def start(cs):
        for c in cs:
            go(c)

    def arrived(cs):
        for c in cs:
            c.wait_recv()

    def add_up(first, ref, n, count):
        value = first
        for k in range(count):
            value = value + ref[n, k]
        return value

    def finish_rs(n, c):
        arrived(c["rs"])
        own = packed[n, pl.ds(pl.multiple_of(f * 8, 8), 8), :]
        part[n, 0] = add_up(own, rs_in, n, 3)

    def finish_x(n, c):
        arrived(c["x"])
        part[n, 1] = add_up(part[n, 0], x_in, n, NX - 1)

    def finish_y(n, c):
        arrived(c["y"])
        part[n, 2] = add_up(part[n, 1], y_in, n, NY - 1)

    def finish_z(n, c):
        arrived(c["z"])
        total[n, 0] = add_up(part[n, 2], z_in, n, NZ - 1)

    def finish_ag(n, c):
        arrived(c["ag"])
        for d in range(4):
            whole[n, pl.ds(pl.multiple_of(mate(d) * 8, 8), 8), :] = total[n, d]

    lane64 = lax.broadcasted_iota(jnp.int32, (K, 2 * K), 1) % K
    row64 = lax.broadcasted_iota(jnp.int32, (K, 2 * K), 0)
    lane1 = lax.broadcasted_iota(jnp.int32, (1, 2 * K), 1) % K

    def invert(n):
        s = whole[n]
        r = pltpu.roll(s, K, 1)
        low = lower_lanes(32)
        full = jnp.concatenate([jnp.where(low, s, r), jnp.where(low, r, s)], axis=0)
        diag = lane64 == row64
        trace = jnp.sum(jnp.where(diag, full, 0.0)) * 0.5
        mean_total = trace / TRAIN
        inv[n] = full / TRAIN + jnp.where(diag, DAMPING * mean_total / K, 0.0)

        def step(k, carry):
            a = inv[n]
            row = inv[n, pl.ds(k, 1), :]
            col = jnp.sum(jnp.where(lane64 == k, a, 0.0), axis=1, keepdims=True) * 0.5
            pivot = jnp.sum(jnp.where(lane1 == k, row, 0.0), axis=1, keepdims=True) * 0.5
            scaled = jnp.where(lane1 == k, 1.0, row) * (1.0 / pivot)
            updated = jnp.where(lane64 == k, 0.0, a) - col * scaled
            inv[n] = jnp.where(row64 == k, scaled, updated)
            return carry

        lax.fori_loop(0, K, step, 0)
        return mean_total

    rcp = 1.0 / cnt[...].astype(F32)
    eye = identity(128)
    for k in range(COLS // 128):
        t = dot_nt(eye, tg[:, k * 128:(k + 1) * 128])
        xto[k * 128:(k + 1) * 128, :] = (t * rcp).astype(BF16)
    g = jnp.zeros((256, 256), F32)
    for k in range(COLS // 256):
        rows = xto[k * 256:(k + 1) * 256, :]
        g = g + dot_nt(rows, rows)
    packed[0] = fold(g)
    c0 = stages(0)
    start(c0["rs"])
    finish_rs(0, c0)
    start(c0["x"])
    finish_x(0, c0)

    to_prev.wait_recv()
    to_prev_ids.wait_recv()

    @pl.when(x == NX - 1)
    def _():
        for c in prev_right:
            c.start()

    @pl.when(x > 0)
    def _():
        for c in prev_left:
            c.start()

    start(c0["y"])
    finish_y(0, c0)
    start(c0["z"])
    finish_z(0, c0)
    start(c0["ag"])
    finish_ag(0, c0)

    invert(0)
    low = lower_lanes(K)
    full = inv[0]
    hi, rest = split(full)
    rest32 = full - hi.astype(F32)
    mid = rest32.astype(BF16)
    tiny = (rest32 - mid.astype(F32)).astype(BF16)
    for n, term in enumerate((hi, mid, tiny)):
        zero = jnp.zeros_like(term)
        rsm[n * 128:n * 128 + 64, :] = jnp.where(low, term, zero)
        rsm[n * 128 + 64:n * 128 + 128, :] = jnp.where(low, zero, term)

    own_lanes = pl.ds(pl.multiple_of(f * PART, PART), PART)
    rcp_part = 1.0 / cnt[:, own_lanes].astype(F32)

    def transpose_half(half):
        scale = rcp_part[:, half * HALF:(half + 1) * HALF]
        for d in range(4):
            base = mate(d) * COLS
            for k in range(COLS // 128):
                cols = slice(k * 128, (k + 1) * 128)
                if d == 0:
                    rows = pl.ds(pl.multiple_of(f * PART + half * HALF, HALF), HALF)
                    block = tg[rows, cols]
                else:
                    block = xr[d - 1, half * HALF:(half + 1) * HALF, cols]
                t = (dot_nt(eye, block) * scale).astype(BF16).astype(F32)
                xt[half, pl.ds(pl.multiple_of(base + k * 128, 128), 128), :] = t

    arrived([regroup[0, d] for d in (1, 2, 3)])
    transpose_half(0)

    for c in own_right:
        c.wait_recv()
    for c in own_left:
        c.wait_recv()
    relay_r = along(2, qall.at[1, 0], ids.at[1], right, at_relay_r)
    relay_l = along(2, qall.at[3, 0], ids.at[3], left, at_relay_l)

    relays = (x == 1) | (x == 2)

    @pl.when(relays)
    def _():
        for c in relay_r + relay_l:
            c.start()

    go(core_a[1])
    go(core_a[3])

    arrived([regroup[1, d] for d in (1, 2, 3)])
    go(z_a[0])
    transpose_half(1)

    def regather(b, carry):
        for half in range(2):
            rows = xt[half, pl.ds(b, K, stride=K), :].astype(BF16)
            xb[pl.ds(pl.multiple_of(b * K, K), K), half * HALF:(half + 1) * HALF] = rows
        return carry

    lax.fori_loop(0, K, regather, 0, unroll=4)

    acc_g = jnp.zeros((256, 256), F32)

    def add_gram(k, total_g):
        rows = xb[pl.ds(pl.multiple_of(k * 256, 256), 256), :]
        return total_g + dot_nt(rows, rows)

    acc_g = lax.fori_loop(0, 16, add_gram, acc_g)
    packed[1] = fold(acc_g)
    c1 = stages(1)
    start(c1["rs"])
    go(z_a[1])
    go(z_a[3])
    finish_rs(1, c1)
    start(c1["x"])

    eye256 = identity(256)

    def put_back(k, carry):
        at = pl.multiple_of(k * 256, 256)
        xbt[:, pl.ds(at, 256)] = dot_nt(eye256, xb[pl.ds(at, 256), :]).astype(BF16)
        return carry

    lax.fori_loop(0, 16, put_back, 0)
    finish_x(1, c1)
    start(c1["y"])
    tcol[...] = jnp.broadcast_to(tid[:, own_lanes], (128, PART)).T
    finish_y(1, c1)
    start(c1["z"])

    @pl.when(x >= 2)
    def _():
        for c in relay_r:
            c.wait_recv()

    @pl.when(x < 2)
    def _():
        for c in relay_l:
            c.wait_recv()

    go(z_a[2])
    go(core_a[2])
    finish_z(1, c1)
    start(c1["ag"])
    finish_ag(1, c1)
    mean_total = invert(1)
    full = inv[1] * mean_total
    hi, lo = split(full)
    lsm[0:64, :] = hi
    lsm[64:128, :] = jnp.where(low, lo, jnp.zeros_like(lo))

    def right_product(s, d):
        base = mate(d) * COLS

        def step(k, carry):
            cols = pl.ds(pl.multiple_of(k * 128, 128), 128)
            t = dot_nt(rsm[...], qall[s, d, :, cols])
            t = t[0:128] + (t[128:256] + t[256:384])
            rows = pl.ds(pl.multiple_of(base + k * 128, 128), 128)
            m[0, rows, :] = t[:, 0:128]
            m[1, rows, 0:64] = t[:, 128:192]
            return carry

        lax.fori_loop(0, COLS // 128, step, 0)

    def regroup_queries(s):
        def step(b, carry):
            at = pl.multiple_of(b * 2 * K, 2 * K)
            for j, lanes in enumerate((128, 64)):
                hi, lo = split(m[j, pl.ds(b, K, stride=K), :][:, 0:lanes])
                w[s, pl.ds(at, K), j * 128:j * 128 + lanes] = hi
                w[s, pl.ds(at + K, K), j * 128:j * 128 + lanes] = lo
            return carry

        lax.fori_loop(0, K, step, 0, unroll=2)

    def scores(s):
        acc[...] = jnp.zeros_like(acc)

        def step(g, carry):
            pieces = []
            for j in range(4):
                at = pl.multiple_of(g * 512 + j * 128, 128)
                t = dot_nn(lsm[...], w[s, pl.ds(at, 128), :])
                pieces.append((t[0:64] + t[64:128]).astype(BF16))
            at = pl.multiple_of(g * 256, 256)
            acc[...] += dot_nn(xbt[:, pl.ds(at, 256)], jnp.concatenate(pieces, axis=0))
            return carry

        lax.fori_loop(0, 16, step, 0)
        same = tcol[:, 0:1] == ids[s, 0:1, 0:QD]
        st[s] = jnp.where(same, 0.0, acc[...]).T

    results = []
    for s in (0, 1, 3, 2):
        core_a[s].wait_recv()
        z_a[s].wait_recv()
        go(core_b[s])
        right_product(s, 0)
        right_product(s, 1)
        right_product(s, 2)
        core_b[s].wait_recv()
        right_product(s, 3)
        regroup_queries(s)
        scores(s)
        for d in (2, 3, 1):
            results.append(go(copy(
                st.at[s, pl.ds(pl.multiple_of(mate(d) * QROWS, 8), QROWS), :],
                out.at[s, :, own_lanes], i, mate(d))))
        out[s, :, own_lanes] = st[s, pl.ds(pl.multiple_of(f * QROWS, 8), QROWS), :]

    for c in results:
        c.wait_recv()
    for c in sent:
        c.wait_send()
    for c in own_right + own_left:
        c.wait_send()

    @pl.when(relays)
    def _():
        for c in relay_r + relay_l:
            c.wait_send()


N_SEM = 80


def on_device(train_grads, token_counts, train_ids, query_grads, query_ids):
    cnt = token_counts.reshape(1, EX)
    tid = train_ids.reshape(1, EX)
    qid = jnp.pad(query_ids, (0, 256 - QD)).reshape(1, 256)
    vmem = pltpu.VMEM
    scratch = [
        vmem((3, PART, COLS), BF16),
        vmem((COLS, EX), BF16),
        vmem((2, K * K, HALF), F32),
        vmem((K * K, PART), BF16),
        vmem((PART, K * K), BF16),
        vmem((STEPS, NF, QD, COLS), BF16),
        vmem((QD, COLS), BF16),
        vmem((STEPS, 8, 256), jnp.int32),
        vmem((8, 256), jnp.int32),
        vmem((2, K * K, 128), F32),
        vmem((STEPS, 2 * K * K, QD), BF16),
        vmem((STEPS, QD, PART), F32),
        vmem((PART, QD), F32),
        vmem((PART, 128), jnp.int32),
        vmem((2, 32, 128), F32),
        vmem((2, 3, 8, 128), F32),
        vmem((2, 3, 8, 128), F32),
        vmem((2, NX - 1, 8, 128), F32),
        vmem((2, NY - 1, 8, 128), F32),
        vmem((2, NZ - 1, 8, 128), F32),
        vmem((2, 4, 8, 128), F32),
        vmem((2, 32, 128), F32),
        vmem((2, K, 2 * K), F32),
        vmem((384, 128), BF16),
        vmem((128, 128), BF16),
        pltpu.SemaphoreType.DMA((N_SEM,)),
        pltpu.SemaphoreType.DMA((N_SEM,)),
        pltpu.SemaphoreType.DMA,
    ]
    spec = pl.BlockSpec(memory_space=pltpu.VMEM)
    return pl.pallas_call(
        kernel,
        out_shape=jax.ShapeDtypeStruct((STEPS, QROWS, EX), F32),
        in_specs=[spec] * 5,
        out_specs=spec,
        scratch_shapes=scratch,
        compiler_params=pltpu.CompilerParams(
            collective_id=0, has_side_effects=True, vmem_limit_bytes=58 * 1024 * 1024
        ),
        cost_estimate=pl.CostEstimate(flops=4_000_000_000, bytes_accessed=8_000_000, transcendentals=0),
    )(train_grads, query_grads, cnt, tid, qid)


def solution(mesh):
    in_specs = (P("dp", "feat"), P("dp"), P("dp"), P("dp", "feat"), P("dp"))
    out_specs = P(None, "feat", "dp")
    return jax.shard_map(
        on_device, mesh=mesh, in_specs=in_specs, out_specs=out_specs, check_vma=False
    )
```

time: 378 us -> 205 us (0.54)
  Pallas kernels: 0 us -> 201 us
  waiting for transfers between devices: 181 us -> 0 us
  blocking collectives: 99.8 us -> 0 us
  other arithmetic: 31.7 us -> 0 us
  starting transfers between devices: 22.8 us -> 0 us
  matrix products: 22.2 us -> 0 us
  between operations: 14.6 us -> 0.01 us
    pallas_call x0 -> x1, Pallas kernels: none -> 201 us  [on_device(): pl.pallas_call(kernel, out_shape=jax.ShapeDtypeStruct((STEPS, QROWS, EX),...]
    psum x1 -> x0, blocking collectives: 99.8 us -> none  [on_device(): lax.psum((right_part, left_part), ('dp', 'feat'))]
    ppermute x6 -> x0, waiting for transfers between devices: 76.1 us -> none  [passed_along(): return lax.ppermute(block, axis, route)]
    reduce_scatter x4 -> x0, waiting for transfers between devices: 75.2 us -> none  [on_device(): lax.psum_scatter(score_tile, 'feat', scatter_dimension=0, tiled=True)]
    all_to_all x1 -> x0, waiting for transfers between devices: 28.2 us -> none  [on_device(): lax.all_to_all(features, 'feat', split_axis=0, concat_axis=1, tiled=True)]
    another operation x11 -> x0, other arithmetic: 26.6 us -> none  [the longest x6 13.2 us: inverse(): factor = jnp.linalg.cholesky(matrix)]
    dot_general x8 -> x0, matrix products: 21.4 us -> none  [the longest x4 12.2 us: on_device(): lax.dot_general(query_block, features, (((1,), (1,)), ((), ())), preferre...]
    ppermute x6 -> x0, starting transfers between devices: 12 us -> none  [passed_along(): return lax.ppermute(block, axis, route)]
  transfers between devices with their start and end apart: 12 -> 0, of which waited for: 9 -> 0; matrix products, arithmetic and copies ran while one was open for 12% -> 0% of each run, Pallas kernels for 0% -> 0%
where the time goes in v1:
time: 205 us; the launch traced here: 204 us
  Pallas kernels  201 us (98%)
  local copies, waits for them, and re-layouts  3.33 us (2%)
    pallas_call x1, Pallas kernels, on_device(): pl.pallas_call(kernel, out_shape=jax.ShapeDtypeStruct((STEPS, QROWS, EX),...  201 us

profile of v1, /device:TPU:1, one launch (start us, length us, event | category | flops | bytes accessed | tf_op | source)
XLA Modules:
  0.0 203.9 jit_solution(12744605728268958235)
XLA Ops:
  0.0 1.2 pad.4
  1.2 200.5 %shard_map.55 = f32[4,48,1024]{2,1,0:T(8,128)} custom-call(bf16[1024,1024]{1,0:T(8,128)(2,1)} %tg.1, bf16[192,1024]{1,0:T(8,128)(2,1)} %qg.1, s32[1,1024]{1,0:T(1,128)} %bitcast.4, s32[1,1024]{1,0:T(1,128)} %bitcast.5, s32[1,256]{1,0:T(1,128)} %bitcast.3), custom_call_target="tpu_custom_call" | custom-call | flops 4000000000 | bytes 8000000 | tf_op jit(solution)/shard_map/pallas_call | solution.py:499
  201.8 2.1 %copy.7 = f32[4,48,1024]{2,1,0:T(8,128)} copy(f32[4,48,1024]{2,1,0:T(8,128)} %shard_map.55) | data formatting | bytes 1572864

commit v2 on v0

v2 whole, which is shorter than its diff:
```python
import jax
import jax.numpy as jnp
from jax import lax
from jax.experimental import pallas as pl
from jax.experimental.pallas import tpu as pltpu
from jax.sharding import PartitionSpec as P

K = 64
PITCH = 72
STEPS = 4
NX, NY, NZ, NF = 4, 8, 4, 4
N_DP = NX * NY * NZ
TRAIN = 131072
EX = 1024
COLS = 1024
PART = EX // NF
HALF = PART // 2
QD = 192
QROWS = QD // NF
DAMPING = 0.1

F32 = jnp.float32
BF16 = jnp.bfloat16


def dot_nt(a, b):
    return lax.dot_general(a, b, (((1,), (1,)), ((), ())), preferred_element_type=F32)


def dot_nn(a, b):
    return lax.dot_general(a, b, (((1,), (0,)), ((), ())), preferred_element_type=F32)


def identity(n):
    rows = lax.broadcasted_iota(jnp.int32, (n, n), 0)
    cols = lax.broadcasted_iota(jnp.int32, (n, n), 1)
    return jnp.where(rows == cols, 1.0, 0.0).astype(BF16)


def lower_lanes(rows):
    return lax.broadcasted_iota(jnp.int32, (rows, 2 * K), 1) < K


def fold(g):
    low = lower_lanes(K)
    h = jnp.where(low, g[0:64, 0:128], g[64:128, 0:128]) + jnp.where(
        low, g[128:192, 128:256], g[192:256, 128:256]
    )
    both = h + pltpu.roll(h, K, 1)
    return jnp.where(lower_lanes(32), both[0:32], both[32:64])


def split(v):
    high = v.astype(BF16)
    return high, (v - high.astype(F32)).astype(BF16)


def kernel(
    tg, qg, cnt, tid, qid, out,
    xr, xto, xt, xb, xbt, qall, prev, hop1, hop2, ids, prev_ids, hop_ids, m, w, st, p, tcol,
    packed, c_in, part, x_in, y_in, z_in, total, other, whole, inv, rsm, lsm,
    send, recv,
):
    f = lax.axis_index("feat")
    i = lax.axis_index("dp")
    x = i % NX
    y = (i // NX) % NY
    zh = i // (NX * NY)
    core = f % 2
    z = 2 * zh + f // 2

    def mate(d):
        if d == 0:
            return f
        if d == 1:
            return f + 1 - 2 * core
        if d == 2:
            return (f + 2) % 4
        return 3 - f

    def on_x(d):
        return i - x + (x + d) % NX, f

    def on_y(d):
        return (zh * NY + (y + d) % NY) * NX + x, f

    def on_z(d):
        there = (z + d) % (2 * NZ)
        return ((there // 2) * NY + y) * NX + x, (there % 2) * 2 + core

    def in_group(d):
        return i, mate(d)

    used = [0]

    def reserve(n=1):
        used[0] += n
        return used[0] - n

    def copy(src, dst, device, at=None, recv_at=None):
        at = reserve() if at is None else at
        recv_at = at if recv_at is None else recv_at
        return pltpu.make_async_remote_copy(
            src_ref=src, dst_ref=dst, send_sem=send.at[at], recv_sem=recv.at[recv_at],
            device_id=device, device_id_type=pl.DeviceIdType.MESH,
        )

    barrier = pltpu.get_barrier_semaphore()
    partners = [in_group(1), in_group(3)]
    partners += [on_x(d) for d in range(1, NX)]
    partners += [on_y(d) for d in range(1, NY)]
    partners += [on_z(d) for d in range(1, 2 * NZ)]
    for device in partners:
        pl.semaphore_signal(barrier, inc=1, device_id=device, device_id_type=pl.DeviceIdType.MESH)
    pl.semaphore_wait(barrier, len(partners))

    sent = []

    def go(c):
        c.start()
        sent.append((None, c))
        return c

    def go_if(cond, cs):
        @pl.when(cond)
        def _():
            for c in cs:
                c.start()

        sent.extend((cond, c) for c in cs)

    def arrived(cs):
        for c in cs:
            c.wait_recv()

    def arrived_if(cond, cs):
        @pl.when(cond)
        def _():
            for c in cs:
                c.wait_recv()

    qall[0, 0] = qg[...]
    ids[0] = jnp.zeros((8, 256), jnp.int32)
    ids[0, :, 0:QD] = jnp.broadcast_to(qid[...], (8, QD))
    core_a = [copy(qall.at[s, 0], qall.at[s, 1], in_group(1)) for s in range(STEPS)]
    core_b = [copy(qall.at[s, 2], qall.at[s, 3], in_group(1)) for s in range(STEPS)]
    z_a = {s: copy(qall.at[s, 0], qall.at[s, 2], in_group(2)) for s in (0, 2)}

    def regroup(half, d):
        rows = pl.ds(pl.multiple_of(mate(d) * PART + half * HALF, HALF), HALF)
        return copy(tg.at[rows, :], xr.at[d - 1, pl.ds(half * HALF, HALF), :], in_group(d))

    regrouped = {(half, d): regroup(half, d) for half in range(2) for d in (2, 3, 1)}

    to_next = [copy(qall.at[0, 2 * n], prev.at[n], on_y(1)) for n in range(2)]
    at_prev_ids = reserve()
    to_next_ids = copy(ids.at[0], prev_ids, on_y(1), None, at_prev_ids)
    wrap_ids_1 = copy(ids.at[0], hop_ids, on_z(2))
    wrap_ids_2 = copy(hop_ids, prev_ids, on_y(1), None, at_prev_ids)
    wrap_1, wrap_2, wrap_3, wrap_in = [], [], [], []
    for n in range(2):
        got = reserve()
        wrap_1.append([
            copy(qall.at[0, 2 * n, :, pl.ds((d - 1) * 128, 128)], hop1.at[n], on_y(d), None, got)
            for d in range(1, NY)])
        wrap_2.append(copy(hop1.at[n], hop2.at[n], on_z(2)))
        first = reserve(NY)
        at = reserve()
        to_first = (zh * NY * NX + x, f)
        lanes = pl.ds(pl.multiple_of(y * 128, 128), 128)
        wrap_3.append(copy(hop2.at[n], prev.at[n, :, lanes], to_first, at, first + y))
        wrap_in.append([
            copy(hop2.at[n], prev.at[n, :, pl.ds(j * 128, 128)], to_first, at, first + j)
            for j in range(1, NY)])

    def send_next(n):
        go_if(y < NY - 1, [to_next[n]])
        go_if(y == NY - 1, wrap_1[n])

        @pl.when(y == NY - 1)
        def _():
            hop1[n] = qall[0, 2 * n, :, (NY - 1) * 128:NY * 128]

    def send_wrap_2(n):
        @pl.when(y < NY - 1)
        def _():
            wrap_1[n][0].wait_recv()

        go(wrap_2[n])

    def send_wrap_3(n):
        wrap_2[n].wait_recv()
        go_if(y > 0, [wrap_3[n]])

        @pl.when(y == 0)
        def _():
            prev[n, :, 0:128] = hop2[n]

    def wait_prev(n):
        arrived_if(y > 0, [to_next[n]])
        arrived_if(y == 0, wrap_in[n])

    right, left = on_x(1), on_x(NX - 1)
    at_right, at_left, at_relay = reserve(2), reserve(2), reserve(2)
    at_ids = reserve(4)
    own_right = [copy(qall.at[0, 2 * n], qall.at[1, 2 * n], right, at_right + n) for n in range(2)]
    prev_right = [copy(prev.at[n], qall.at[1, 2 * n], right, at_right + n) for n in range(2)]
    own_left = [copy(qall.at[0, 2 * n], qall.at[3, 2 * n], left, at_left + n) for n in range(2)]
    prev_left = [copy(prev.at[n], qall.at[3, 2 * n], left, at_left + n) for n in range(2)]
    own_right_ids = copy(ids.at[0], ids.at[1], right, at_ids)
    prev_right_ids = copy(prev_ids, ids.at[1], right, at_ids)
    own_left_ids = copy(ids.at[0], ids.at[3], left, at_ids + 1)
    prev_left_ids = copy(prev_ids, ids.at[3], left, at_ids + 1)
    relay_r = [copy(qall.at[1, 0], qall.at[2, 0], right, at_relay),
               copy(ids.at[1], ids.at[2], right, at_ids + 2)]
    relay_l = [copy(qall.at[3, 0], qall.at[2, 0], left, at_relay + 1),
               copy(ids.at[3], ids.at[2], left, at_ids + 3)]
    relays = (x == 1) | (x == 2)

    def send_own(n):
        more = n == 0
        go_if(x < NX - 1, [own_right[n]] + [own_right_ids] * more)
        go_if(x == 0, [own_left[n]] + [own_left_ids] * more)

    def send_prev(n):
        more = n == 0
        go_if(x == NX - 1, [prev_right[n]] + [prev_right_ids] * more)
        go_if(x > 0, [prev_left[n]] + [prev_left_ids] * more)

    class Sum:
        def __init__(self, n):
            self.n = n
            self.mine = pl.ds(pl.multiple_of(core * 16, 16), 16)
            self.theirs = pl.ds(pl.multiple_of((1 - core) * 16, 16), 16)
            self.c = copy(packed.at[n, self.theirs, :], c_in.at[n], in_group(1))
            self.x = [copy(part.at[n, 0], x_in.at[n, d - 1], on_x(d)) for d in range(1, NX)]
            self.y = [copy(part.at[n, 1], y_in.at[n, d - 1], on_y(d)) for d in range(1, NY)]
            self.z = [copy(part.at[n, 2], z_in.at[n, d - 1], on_z(d)) for d in range(1, 2 * NZ)]
            self.back = copy(total.at[n], other.at[n], in_group(1))

        def send(self, cs):
            for c in cs:
                go(c)

        def collect(self, cs, first, ref):
            arrived(cs)
            value = first
            for k in range(len(cs)):
                value = value + ref[self.n, k]
            return value

        def start(self):
            go(self.c)

        def start_x(self):
            self.c.wait_recv()
            part[self.n, 0] = packed[self.n, self.mine, :] + c_in[self.n]
            self.send(self.x)

        def start_y(self):
            part[self.n, 1] = self.collect(self.x, part[self.n, 0], x_in)
            self.send(self.y)

        def start_z(self):
            part[self.n, 2] = self.collect(self.y, part[self.n, 1], y_in)
            self.send(self.z)

        def start_back(self):
            total[self.n] = self.collect(self.z, part[self.n, 2], z_in)
            go(self.back)

        def finish(self):
            self.back.wait_recv()
            whole[self.n, self.mine, :] = total[self.n]
            whole[self.n, self.theirs, :] = other[self.n]

    tile = (8, 8, 128)
    lane64 = lax.broadcasted_iota(jnp.int32, (K, 2 * K), 1) % K
    row64 = lax.broadcasted_iota(jnp.int32, (K, 2 * K), 0)
    lane8 = lax.broadcasted_iota(jnp.int32, (8, 2 * K), 1) % K
    row_of = row64.reshape(tile)
    low = lower_lanes(K)

    def invert(n):
        s = whole[n]
        r = pltpu.roll(s, K, 1)
        low32 = lower_lanes(32)
        full = jnp.concatenate([jnp.where(low32, s, r), jnp.where(low32, r, s)], axis=0)
        diag = lane64 == row64
        trace = jnp.sum(jnp.where(diag, full, 0.0)) * 0.5
        mean_total = trace / TRAIN
        inv[n] = full / TRAIN + jnp.where(diag, DAMPING * mean_total / K, 0.0)
        for k in range(0, K, 4):
            a = inv[n]
            spots = [jnp.full((8, 128), k + j, jnp.int32) for j in range(4)]
            rows = [jnp.broadcast_to(inv[n, k + j:k + j + 1, :], (8, 128)) for j in range(4)]
            e = [[jnp.take_along_axis(rows[j], spots[t], axis=1) for t in range(4)] for j in range(4)]
            cols = [
                jnp.take_along_axis(a, jnp.full((K, 128), k + j, jnp.int32), axis=1).reshape(tile)
                for j in range(4)]
            for t in range(4):
                pivot = 1.0 / e[t][t]
                here = lane8 == k + t
                rows[t] = jnp.where(here, 1.0, rows[t]) * pivot
                scaled = [e[t][v] * pivot for v in range(4)]
                for j in range(4):
                    if j != t:
                        rows[j] = jnp.where(here, 0.0, rows[j]) - e[j][t] * rows[t]
                        for v in range(t + 1, 4):
                            e[j][v] = e[j][v] - e[j][t] * scaled[v]
                for v in range(t + 1, 4):
                    e[t][v] = scaled[v]
            inside = (lane8 >= k) & (lane8 < k + 4)
            u = jnp.where(inside[None], 0.0, a.reshape(tile))
            for j in range(4):
                u = u - cols[j] * rows[j][None]
            for j in range(4):
                u = jnp.where(row_of == k + j, rows[j][None], u)
            inv[n] = u.reshape(K, 2 * K)
        return mean_total

    eye = identity(128)
    own_lanes = pl.ds(pl.multiple_of(f * PART, PART), PART)
    rcp_part = 1.0 / cnt[:, own_lanes].astype(F32)

    def transpose(half, d):
        scale = rcp_part[:, half * HALF:(half + 1) * HALF]
        base = mate(d) * (COLS // K * PITCH)
        for k in range(COLS // 128):
            cols = slice(k * 128, (k + 1) * 128)
            if d == 0:
                rows = pl.ds(pl.multiple_of(f * PART + half * HALF, HALF), HALF)
                block = tg[rows, cols]
            else:
                block = xr[d - 1, half * HALF:(half + 1) * HALF, cols]
            t = (dot_nt(eye, block) * scale).astype(BF16).astype(F32)
            for j in range(2):
                xt[half, pl.ds(pl.multiple_of(base + (2 * k + j) * PITCH, 8), K), :] = t[j * K:(j + 1) * K]

    def right_product(s, d):
        base = mate(d) * (COLS // K * PITCH)
        for k in range(COLS // 128):
            t = dot_nt(rsm[...], qall[s, d, :, k * 128:(k + 1) * 128])
            t = t[0:128] + (t[128:256] + t[256:384])
            for j in range(2):
                rows = pl.ds(pl.multiple_of(base + (2 * k + j) * PITCH, 8), K)
                m[0, rows, :] = t[j * K:(j + 1) * K, 0:128]
                m[1, rows, 0:64] = t[j * K:(j + 1) * K, 128:192]

    def prepare(s):
        for d in range(4):
            right_product(s, d)

        def step(b, carry):
            at = pl.multiple_of(b * 2 * K, 2 * K)
            for j, lanes in enumerate((128, 64)):
                hi, lo = split(m[j, pl.ds(b, K, stride=PITCH), :][:, 0:lanes])
                w[s, pl.ds(at, K), j * 128:j * 128 + lanes] = hi
                w[s, pl.ds(at + K, K), j * 128:j * 128 + lanes] = lo
            return carry

        lax.fori_loop(0, K, step, 0, unroll=8)

    def scores(s):
        def step(b, carry):
            at = pl.multiple_of(b * 128, 128)
            t = dot_nn(lsm[...], w[s, pl.ds(at, 128), :])
            p[pl.ds(pl.multiple_of(b * K, K), K), :] = (t[0:64] + t[64:128]).astype(BF16)
            return carry

        lax.fori_loop(0, K, step, 0, unroll=32)
        value = dot_nn(xbt[...], p[...])
        same = tcol[:, 0:1] == ids[s, 0:1, 0:QD]
        st[s] = jnp.where(same, 0.0, value).T

    results = []

    def hand_out(s):
        for d in (2, 3, 1):
            results.append(go(copy(
                st.at[s, pl.ds(pl.multiple_of(mate(d) * QROWS, 8), QROWS), :],
                out.at[s, :, own_lanes], in_group(d))))
        out[s, :, own_lanes] = st[s, pl.ds(pl.multiple_of(f * QROWS, 8), QROWS), :]

    go(z_a[0])
    go(regrouped[0, 2])
    go(regrouped[0, 3])
    go(core_a[0])
    go(regrouped[0, 1])
    go(regrouped[1, 1])
    send_next(0)
    go_if(y < NY - 1, [to_next_ids])
    go_if(y == NY - 1, [wrap_ids_1])

    rcp = 1.0 / cnt[...].astype(F32)
    for k in range(COLS // 128):
        t = dot_nt(eye, tg[:, k * 128:(k + 1) * 128])
        xto[k * 128:(k + 1) * 128, :] = (t * rcp).astype(BF16)
    g = jnp.zeros((256, 256), F32)
    for k in range(COLS // 256):
        rows = xto[k * 256:(k + 1) * 256, :]
        g = g + dot_nt(rows, rows)
    packed[0] = fold(g)
    sum0 = Sum(0)
    sum0.start()
    sum0.start_x()
    send_own(0)
    send_wrap_2(0)
    transpose(0, 0)
    transpose(1, 0)
    tcol[...] = jnp.broadcast_to(tid[:, own_lanes], (128, PART)).T
    arrived([regrouped[0, 1], regrouped[1, 1]])
    transpose(0, 1)
    transpose(1, 1)
    send_wrap_3(0)
    sum0.start_y()
    z_a[0].wait_recv()
    send_next(1)
    send_own(1)
    go(core_b[0])
    arrived_if(y == NY - 1, [wrap_ids_1])
    go_if(y == NY - 1, [wrap_ids_2])
    wait_prev(0)
    to_next_ids.wait_recv()
    send_prev(0)
    sum0.start_z()
    go(regrouped[1, 2])
    go(regrouped[1, 3])
    send_wrap_2(1)
    arrived([own_right[0], own_left[0], own_right_ids, own_left_ids])
    go_if(relays, relay_r + relay_l)
    go(core_a[1])
    go(core_a[3])
    send_wrap_3(1)
    wait_prev(1)
    send_prev(1)
    arrived([regrouped[0, 2], regrouped[0, 3]])
    transpose(0, 2)
    transpose(0, 3)
    sum0.start_back()
    sum0.finish()
    invert(0)
    full = inv[0]
    hi = full.astype(BF16)
    rest = full - hi.astype(F32)
    mid, tiny = split(rest)
    zero = jnp.zeros_like(hi)
    for n, term in enumerate((hi, mid, tiny)):
        rsm[n * 128:n * 128 + 64, :] = jnp.where(low, term, zero)
        rsm[n * 128 + 64:n * 128 + 128, :] = jnp.where(low, zero, term)
    arrived([core_a[0], core_b[0]])
    prepare(0)
    arrived([own_right[1], own_left[1]])
    go(core_b[1])
    go(core_b[3])

    arrived([regrouped[1, 2], regrouped[1, 3]])
    transpose(1, 2)
    transpose(1, 3)

    def regather(b, carry):
        for half in range(2):
            rows = xt[half, pl.ds(b, K, stride=PITCH), :].astype(BF16)
            xb[pl.ds(pl.multiple_of(b * K, K), K), half * HALF:(half + 1) * HALF] = rows
        return carry

    lax.fori_loop(0, K, regather, 0, unroll=8)

    def add_gram(k, total_g):
        rows = xb[pl.ds(pl.multiple_of(k * 256, 256), 256), :]
        return total_g + dot_nt(rows, rows)

    packed[1] = fold(lax.fori_loop(0, 16, add_gram, jnp.zeros((256, 256), F32), unroll=4))
    sum1 = Sum(1)
    sum1.start()
    sum1.start_x()
    eye256 = identity(256)

    def put_back(k, carry):
        at = pl.multiple_of(k * 256, 256)
        xbt[:, pl.ds(at, 256)] = dot_nt(eye256, xb[pl.ds(at, 256), :]).astype(BF16)
        return carry

    lax.fori_loop(0, 16, put_back, 0, unroll=4)
    arrived_if(x >= 2, relay_r)
    arrived_if(x < 2, relay_l)
    go(z_a[2])
    go(core_a[2])
    sum1.start_y()
    arrived([core_a[1], core_b[1]])
    prepare(1)
    sum1.start_z()
    arrived([core_a[3], core_b[3]])
    prepare(3)
    sum1.start_back()
    sum1.finish()
    mean_total = invert(1)
    hi, lo = split(inv[1] * mean_total)
    lsm[0:64, :] = hi
    lsm[64:128, :] = jnp.where(low, lo, jnp.zeros_like(lo))

    z_a[2].wait_recv()
    go(core_b[2])
    scores(0)
    hand_out(0)
    scores(1)
    hand_out(1)
    scores(3)
    hand_out(3)
    arrived([core_a[2], core_b[2]])
    prepare(2)
    scores(2)
    hand_out(2)

    assert used[0] <= N_SEM, used
    arrived(results)
    for cond, c in sent:
        if cond is None:
            c.wait_send()
    for cond, c in sent:
        if cond is not None:
            pl.when(cond)(c.wait_send)


N_SEM = 136


def on_device(train_grads, token_counts, train_ids, query_grads, query_ids):
    cnt = token_counts.reshape(1, EX)
    tid = train_ids.reshape(1, EX)
    qid = query_ids.reshape(1, QD)
    vmem = pltpu.VMEM
    scratch = [
        vmem((3, PART, COLS), BF16),
        vmem((COLS, EX), BF16),
        vmem((2, K * PITCH, HALF), F32),
        vmem((K * K, PART), BF16),
        vmem((PART, K * K), BF16),
        vmem((STEPS, NF, QD, COLS), BF16),
        vmem((2, QD, COLS), BF16),
        vmem((2, QD, 128), BF16),
        vmem((2, QD, 128), BF16),
        vmem((STEPS, 8, 256), jnp.int32),
        vmem((8, 256), jnp.int32),
        vmem((8, 256), jnp.int32),
        vmem((2, K * PITCH, 128), F32),
        vmem((STEPS, 2 * K * K, QD), BF16),
        vmem((STEPS, QD, PART), F32),
        vmem((K * K, QD), BF16),
        vmem((PART, 128), jnp.int32),
        vmem((2, 32, 128), F32),
        vmem((2, 16, 128), F32),
        vmem((2, 3, 16, 128), F32),
        vmem((2, NX - 1, 16, 128), F32),
        vmem((2, NY - 1, 16, 128), F32),
        vmem((2, 2 * NZ - 1, 16, 128), F32),
        vmem((2, 16, 128), F32),
        vmem((2, 16, 128), F32),
        vmem((2, 32, 128), F32),
        vmem((2, K, 2 * K), F32),
        vmem((384, 128), BF16),
        vmem((128, 128), BF16),
        pltpu.SemaphoreType.DMA((N_SEM,)),
        pltpu.SemaphoreType.DMA((N_SEM,)),
    ]
    spec = pl.BlockSpec(memory_space=pltpu.VMEM)
    return pl.pallas_call(
        kernel,
        out_shape=jax.ShapeDtypeStruct((STEPS, QROWS, EX), F32),
        in_specs=[spec] * 5,
        out_specs=spec,
        scratch_shapes=scratch,
        compiler_params=pltpu.CompilerParams(
            collective_id=0, has_side_effects=True, vmem_limit_bytes=58 * 1024 * 1024
        ),
        cost_estimate=pl.CostEstimate(flops=4_000_000_000, bytes_accessed=8_000_000, transcendentals=0),
    )(train_grads, query_grads, cnt, tid, qid)


def solution(mesh):
    in_specs = (P("dp", "feat"), P("dp"), P("dp"), P("dp", "feat"), P("dp"))
    out_specs = P(None, "feat", "dp")
    return jax.shard_map(
        on_device, mesh=mesh, in_specs=in_specs, out_specs=out_specs, check_vma=False
    )
```

time: 378 us -> 121 us (0.32)
  waiting for transfers between devices: 181 us -> 0 us
  Pallas kernels: 0 us -> 119 us
  blocking collectives: 99.8 us -> 0 us
  other arithmetic: 31.7 us -> 0 us
  starting transfers between devices: 22.8 us -> 0 us
  matrix products: 22.2 us -> 0 us
  between operations: 14.6 us -> 0.01 us
    pallas_call x0 -> x1, Pallas kernels: none -> 119 us  [on_device(): pl.pallas_call(kernel, out_shape=jax.ShapeDtypeStruct((STEPS, QROWS, EX),...]
    psum x1 -> x0, blocking collectives: 99.8 us -> none  [on_device(): lax.psum((right_part, left_part), ('dp', 'feat'))]
    ppermute x6 -> x0, waiting for transfers between devices: 76.1 us -> none  [passed_along(): return lax.ppermute(block, axis, route)]
    reduce_scatter x4 -> x0, waiting for transfers between devices: 75.2 us -> none  [on_device(): lax.psum_scatter(score_tile, 'feat', scatter_dimension=0, tiled=True)]
    all_to_all x1 -> x0, waiting for transfers between devices: 28.2 us -> none  [on_device(): lax.all_to_all(features, 'feat', split_axis=0, concat_axis=1, tiled=True)]
    another operation x11 -> x0, other arithmetic: 26.6 us -> none  [the longest x6 13.2 us: inverse(): factor = jnp.linalg.cholesky(matrix)]
    dot_general x8 -> x0, matrix products: 21.4 us -> none  [the longest x4 12.2 us: on_device(): lax.dot_general(query_block, features, (((1,), (1,)), ((), ())), preferre...]
    ppermute x6 -> x0, starting transfers between devices: 12 us -> none  [passed_along(): return lax.ppermute(block, axis, route)]
  transfers between devices with their start and end apart: 12 -> 0, of which waited for: 9 -> 0; matrix products, arithmetic and copies ran while one was open for 12% -> 0% of each run, Pallas kernels for 0% -> 0%
where the time goes in v2:
time: 121 us
  Pallas kernels  119 us (98%)
  local copies, waits for them, and re-layouts  2.09 us (2%)
    pallas_call x1, Pallas kernels, on_device(): pl.pallas_call(kernel, out_shape=jax.ShapeDtypeStruct((STEPS, QROWS, EX),...  119 us

profile of v2, /device:TPU:1, one launch (start us, length us, event | category | flops | bytes accessed | tf_op | source)
XLA Modules:
  0.0 121.0 jit_solution(8670185995887416604)
XLA Ops:
  0.0 118.9 %shard_map.55 = f32[4,48,1024]{2,1,0:T(8,128)} custom-call(bf16[1024,1024]{1,0:T(8,128)(2,1)} %tg.1, bf16[192,1024]{1,0:T(8,128)(2,1)} %qg.1, s32[1,1024]{1,0:T(1,128)} %bitcast.3, s32[1,1024]{1,0:T(1,128)} %bitcast.4, s32[1,192]{1,0:T(1,128)} %bitcast.5), custom_call_target="tpu_custom_call" | custom-call | flops 4000000000 | bytes 8000000 | tf_op jit(solution)/shard_map/pallas_call | solution.py:567
  118.9 2.1 %copy.7 = f32[4,48,1024]{2,1,0:T(8,128)} copy(f32[4,48,1024]{2,1,0:T(8,128)} %shard_map.55) | data formatting | bytes 1572864

commit v3 on v2

--- a/solution.py
+++ b/solution.py
@@ -157,13 +157,13 @@
     to_next_ids = copy(ids.at[0], prev_ids, on_y(1), None, at_prev_ids)
     wrap_ids_1 = copy(ids.at[0], hop_ids, on_z(2))
     wrap_ids_2 = copy(hop_ids, prev_ids, on_y(1), None, at_prev_ids)
-    wrap_1, wrap_2, wrap_3, wrap_in = [], [], [], []
+    got = reserve()
+    wrap_1 = [
+        copy(qall.at[0, 0, :, pl.ds((d - 1) * 128, 128)], hop1, on_y(d), None, got)
+        for d in range(1, NY)]
+    wrap_2 = [copy(hop1, hop2.at[0], on_z(2)), copy(hop1, hop2.at[1], on_z(3 - 2 * (f // 2)))]
+    wrap_3, wrap_in = [], []
     for n in range(2):
-        got = reserve()
-        wrap_1.append([
-            copy(qall.at[0, 2 * n, :, pl.ds((d - 1) * 128, 128)], hop1.at[n], on_y(d), None, got)
-            for d in range(1, NY)])
-        wrap_2.append(copy(hop1.at[n], hop2.at[n], on_z(2)))
         first = reserve(NY)
         at = reserve()
         to_first = (zh * NY * NX + x, f)
@@ -175,26 +175,30 @@
 
     def send_next(n):
         go_if(y < NY - 1, [to_next[n]])
-        go_if(y == NY - 1, wrap_1[n])
+
+    def send_wrap_1():
+        go_if(y == NY - 1, wrap_1)
 
         @pl.when(y == NY - 1)
         def _():
-            hop1[n] = qall[0, 2 * n, :, (NY - 1) * 128:NY * 128]
-
-    def send_wrap_2(n):
+            hop1[...] = qall[0, 0, :, (NY - 1) * 128:NY * 128]
+
+    def send_wrap_2():
         @pl.when(y < NY - 1)
         def _():
-            wrap_1[n][0].wait_recv()
-
-        go(wrap_2[n])
-
-    def send_wrap_3(n):
-        wrap_2[n].wait_recv()
-        go_if(y > 0, [wrap_3[n]])
+            wrap_1[0].wait_recv()
+
+        for c in wrap_2:
+            go(c)
+
+    def send_wrap_3():
+        arrived(wrap_2)
+        go_if(y > 0, wrap_3)
 
         @pl.when(y == 0)
         def _():
-            prev[n, :, 0:128] = hop2[n]
+            for n in range(2):
+                prev[n, :, 0:128] = hop2[n]
 
     def wait_prev(n):
         arrived_if(y > 0, [to_next[n]])
@@ -347,16 +351,18 @@
                 m[0, rows, :] = t[j * K:(j + 1) * K, 0:128]
                 m[1, rows, 0:64] = t[j * K:(j + 1) * K, 128:192]
 
-    def prepare(s):
-        for d in range(4):
+    def prepare(s, pieces):
+        for d in pieces:
             right_product(s, d)
 
         def step(b, carry):
-            at = pl.multiple_of(b * 2 * K, 2 * K)
-            for j, lanes in enumerate((128, 64)):
-                hi, lo = split(m[j, pl.ds(b, K, stride=PITCH), :][:, 0:lanes])
-                w[s, pl.ds(at, K), j * 128:j * 128 + lanes] = hi
-                w[s, pl.ds(at + K, K), j * 128:j * 128 + lanes] = lo
+            for d in pieces:
+                start = mate(d) * (COLS // K * PITCH)
+                at = pl.multiple_of(b * 2 * K + mate(d) * 16, 16)
+                for j, lanes in enumerate((128, 64)):
+                    hi, lo = split(m[j, pl.ds(start + b, 16, stride=PITCH), :][:, 0:lanes])
+                    w[s, pl.ds(at, 16), j * 128:j * 128 + lanes] = hi
+                    w[s, pl.ds(at + K, 16), j * 128:j * 128 + lanes] = lo
             return carry
 
         lax.fori_loop(0, K, step, 0, unroll=8)
@@ -382,12 +388,11 @@
                 out.at[s, :, own_lanes], in_group(d))))
         out[s, :, own_lanes] = st[s, pl.ds(pl.multiple_of(f * QROWS, 8), QROWS), :]
 
-    go(z_a[0])
     go(regrouped[0, 2])
-    go(regrouped[0, 3])
     go(core_a[0])
     go(regrouped[0, 1])
     go(regrouped[1, 1])
+    send_wrap_1()
     send_next(0)
     go_if(y < NY - 1, [to_next_ids])
     go_if(y == NY - 1, [wrap_ids_1])
@@ -405,38 +410,53 @@
     sum0.start()
     sum0.start_x()
     send_own(0)
-    send_wrap_2(0)
+    send_wrap_2()
+    go(regrouped[0, 3])
+    go(regrouped[1, 2])
+    go(regrouped[1, 3])
     transpose(0, 0)
     transpose(1, 0)
     tcol[...] = jnp.broadcast_to(tid[:, own_lanes], (128, PART)).T
+    sum0.start_y()
+    arrived_if(y == NY - 1, [wrap_ids_1])
+    go_if(y == NY - 1, [wrap_ids_2])
+    send_wrap_3()
+    wait_prev(0)
+    to_next_ids.wait_recv()
+    send_prev(0)
     arrived([regrouped[0, 1], regrouped[1, 1]])
     transpose(0, 1)
     transpose(1, 1)
-    send_wrap_3(0)
-    sum0.start_y()
-    z_a[0].wait_recv()
-    send_next(1)
-    send_own(1)
-    go(core_b[0])
-    arrived_if(y == NY - 1, [wrap_ids_1])
-    go_if(y == NY - 1, [wrap_ids_2])
-    wait_prev(0)
-    to_next_ids.wait_recv()
-    send_prev(0)
     sum0.start_z()
-    go(regrouped[1, 2])
-    go(regrouped[1, 3])
-    send_wrap_2(1)
+    go(z_a[0])
+    arrived([regrouped[0, 2], regrouped[0, 3]])
+    transpose(0, 2)
+    transpose(0, 3)
     arrived([own_right[0], own_left[0], own_right_ids, own_left_ids])
     go_if(relays, relay_r + relay_l)
     go(core_a[1])
     go(core_a[3])
-    send_wrap_3(1)
-    wait_prev(1)
-    send_prev(1)
-    arrived([regrouped[0, 2], regrouped[0, 3]])
-    transpose(0, 2)
-    transpose(0, 3)
+
+    arrived([regrouped[1, 2], regrouped[1, 3]])
+    transpose(1, 2)
+    transpose(1, 3)
+
+    def regather(b, carry):
+        for half in range(2):
+            rows = xt[half, pl.ds(b, K, stride=PITCH), :].astype(BF16)
+            xb[pl.ds(pl.multiple_of(b * K, K), K), half * HALF:(half + 1) * HALF] = rows
+        return carry
+
+    lax.fori_loop(0, K, regather, 0, unroll=8)
+
+    def add_gram(k, total_g):
+        rows = xb[pl.ds(pl.multiple_of(k * 256, 256), 256), :]
+        return total_g + dot_nt(rows, rows)
+
+    packed[1] = fold(lax.fori_loop(0, 16, add_gram, jnp.zeros((256, 256), F32), unroll=4))
+    sum1 = Sum(1)
+    sum1.start()
+    sum1.start_x()
     sum0.start_back()
     sum0.finish()
     invert(0)
@@ -448,32 +468,11 @@
     for n, term in enumerate((hi, mid, tiny)):
         rsm[n * 128:n * 128 + 64, :] = jnp.where(low, term, zero)
         rsm[n * 128 + 64:n * 128 + 128, :] = jnp.where(low, zero, term)
-    arrived([core_a[0], core_b[0]])
-    prepare(0)
-    arrived([own_right[1], own_left[1]])
-    go(core_b[1])
-    go(core_b[3])
-
-    arrived([regrouped[1, 2], regrouped[1, 3]])
-    transpose(1, 2)
-    transpose(1, 3)
-
-    def regather(b, carry):
-        for half in range(2):
-            rows = xt[half, pl.ds(b, K, stride=PITCH), :].astype(BF16)
-            xb[pl.ds(pl.multiple_of(b * K, K), K), half * HALF:(half + 1) * HALF] = rows
-        return carry
-
-    lax.fori_loop(0, K, regather, 0, unroll=8)
-
-    def add_gram(k, total_g):
-        rows = xb[pl.ds(pl.multiple_of(k * 256, 256), 256), :]
-        return total_g + dot_nt(rows, rows)
-
-    packed[1] = fold(lax.fori_loop(0, 16, add_gram, jnp.zeros((256, 256), F32), unroll=4))
-    sum1 = Sum(1)
-    sum1.start()
-    sum1.start_x()
+    sum1.start_y()
+    z_a[0].wait_recv()
+    send_next(1)
+    send_own(1)
+    go(core_b[0])
     eye256 = identity(256)
 
     def put_back(k, carry):
@@ -482,37 +481,44 @@
         return carry
 
     lax.fori_loop(0, 16, put_back, 0, unroll=4)
+    sum1.start_z()
     arrived_if(x >= 2, relay_r)
     arrived_if(x < 2, relay_l)
     go(z_a[2])
     go(core_a[2])
-    sum1.start_y()
-    arrived([core_a[1], core_b[1]])
-    prepare(1)
-    sum1.start_z()
-    arrived([core_a[3], core_b[3]])
-    prepare(3)
+    arrived([core_a[0], core_b[0]])
+    prepare(0, (0, 1, 2, 3))
+    wait_prev(1)
+    send_prev(1)
     sum1.start_back()
+    arrived([core_a[1], core_a[3]])
+    prepare(1, (0, 1))
     sum1.finish()
     mean_total = invert(1)
     hi, lo = split(inv[1] * mean_total)
     lsm[0:64, :] = hi
     lsm[64:128, :] = jnp.where(low, lo, jnp.zeros_like(lo))
 
+    scores(0)
+    hand_out(0)
+    core_a[2].wait_recv()
+    prepare(2, (0, 1))
     z_a[2].wait_recv()
     go(core_b[2])
-    scores(0)
-    hand_out(0)
-    scores(1)
-    hand_out(1)
-    scores(3)
-    hand_out(3)
-    arrived([core_a[2], core_b[2]])
-    prepare(2)
+    prepare(3, (0, 1))
+    core_b[2].wait_recv()
+    prepare(2, (2, 3))
+    arrived([own_right[1], own_left[1]])
+    go(core_b[1])
+    go(core_b[3])
     scores(2)
     hand_out(2)
-
-    assert used[0] <= N_SEM, used
+    for s in (1, 3):
+        core_b[s].wait_recv()
+        prepare(s, (2, 3))
+        scores(s)
+        hand_out(s)
+
     arrived(results)
     for cond, c in sent:
         if cond is None:
@@ -538,7 +544,7 @@
         vmem((PART, K * K), BF16),
         vmem((STEPS, NF, QD, COLS), BF16),
         vmem((2, QD, COLS), BF16),
-        vmem((2, QD, 128), BF16),
+        vmem((QD, 128), BF16),
         vmem((2, QD, 128), BF16),
         vmem((STEPS, 8, 256), jnp.int32),
         vmem((8, 256), jnp.int32),

time: 121 us -> 98.2 us (0.81)
  Pallas kernels: 119 us -> 95.9 us
    pallas_call x1, Pallas kernels: 119 us -> 95.9 us  [on_device(): pl.pallas_call(kernel, out_shape=jax.ShapeDtypeStruct((STEPS, QROWS, EX),...]
where the time goes in v3:
time: 98.2 us; the launch traced here: 98 us
  Pallas kernels  95.9 us (98%)
  local copies, waits for them, and re-layouts  2.09 us (2%)
    pallas_call x1, Pallas kernels, on_device(): pl.pallas_call(kernel, out_shape=jax.ShapeDtypeStruct((STEPS, QROWS, EX),...  95.9 us
    unnamed x1, local copies, waits for them, and re-layouts  2.09 us

profile of v3, /device:TPU:1, one launch (start us, length us, event | category | flops | bytes accessed | tf_op | source)
XLA Modules:
  0.0 98.0 jit_solution(10441888595705916277)
XLA Ops:
  0.0 95.9 %shard_map.55 = f32[4,48,1024]{2,1,0:T(8,128)} custom-call(bf16[1024,1024]{1,0:T(8,128)(2,1)} %tg.1, bf16[192,1024]{1,0:T(8,128)(2,1)} %qg.1, s32[1,1024]{1,0:T(1,128)} %bitcast.3, s32[1,1024]{1,0:T(1,128)} %bitcast.4, s32[1,192]{1,0:T(1,128)} %bitcast.5), custom_call_target="tpu_custom_call" | custom-call | flops 4000000000 | bytes 8000000 | tf_op jit(solution)/shard_map/pallas_call | solution.py:573
  95.9 2.1 %copy.7 = f32[4,48,1024]{2,1,0:T(8,128)} copy(f32[4,48,1024]{2,1,0:T(8,128)} %shard_map.55) | data formatting | bytes 1572864

commit v4 on v3

--- a/solution.py
+++ b/solution.py
@@ -58,7 +58,7 @@
 def kernel(
     tg, qg, cnt, tid, qid, out,
     xr, xto, xt, xb, xbt, qall, prev, hop1, hop2, ids, prev_ids, hop_ids, m, w, st, p, tcol,
-    packed, c_in, part, x_in, y_in, z_in, total, other, whole, inv, rsm, lsm,
+    packed, c_in, part, x_in, y_in, z_in, total, other, whole, inv, rsm, lsm, gram,
     send, recv,
 ):
     f = lax.axis_index("feat")
@@ -152,7 +152,7 @@
 
     regrouped = {(half, d): regroup(half, d) for half in range(2) for d in (2, 3, 1)}
 
-    to_next = [copy(qall.at[0, 2 * n], prev.at[n], on_y(1)) for n in range(2)]
+    to_next = copy(qall.at[0, 0], prev.at[0], on_y(1))
     at_prev_ids = reserve()
     to_next_ids = copy(ids.at[0], prev_ids, on_y(1), None, at_prev_ids)
     wrap_ids_1 = copy(ids.at[0], hop_ids, on_z(2))
@@ -173,9 +173,6 @@
             copy(hop2.at[n], prev.at[n, :, pl.ds(j * 128, 128)], to_first, at, first + j)
             for j in range(1, NY)])
 
-    def send_next(n):
-        go_if(y < NY - 1, [to_next[n]])
-
     def send_wrap_1():
         go_if(y == NY - 1, wrap_1)
 
@@ -200,36 +197,49 @@
             for n in range(2):
                 prev[n, :, 0:128] = hop2[n]
 
-    def wait_prev(n):
-        arrived_if(y > 0, [to_next[n]])
-        arrived_if(y == 0, wrap_in[n])
+    def wait_prev():
+        arrived_if(y > 0, [to_next])
+        arrived_if(y == 0, wrap_in[0])
 
     right, left = on_x(1), on_x(NX - 1)
-    at_right, at_left, at_relay = reserve(2), reserve(2), reserve(2)
+    at_right, at_left, at_relay = reserve(), reserve(), reserve(2)
     at_ids = reserve(4)
-    own_right = [copy(qall.at[0, 2 * n], qall.at[1, 2 * n], right, at_right + n) for n in range(2)]
-    prev_right = [copy(prev.at[n], qall.at[1, 2 * n], right, at_right + n) for n in range(2)]
-    own_left = [copy(qall.at[0, 2 * n], qall.at[3, 2 * n], left, at_left + n) for n in range(2)]
-    prev_left = [copy(prev.at[n], qall.at[3, 2 * n], left, at_left + n) for n in range(2)]
+    own_right = copy(qall.at[0, 0], qall.at[1, 0], right, at_right)
+    prev_right = copy(prev.at[0], qall.at[1, 0], right, at_right)
+    own_left = copy(qall.at[0, 0], qall.at[3, 0], left, at_left)
+    prev_left = copy(prev.at[0], qall.at[3, 0], left, at_left)
     own_right_ids = copy(ids.at[0], ids.at[1], right, at_ids)
     prev_right_ids = copy(prev_ids, ids.at[1], right, at_ids)
     own_left_ids = copy(ids.at[0], ids.at[3], left, at_ids + 1)
     prev_left_ids = copy(prev_ids, ids.at[3], left, at_ids + 1)
+    parts = [pl.ds(0, QD // 2), pl.ds(QD // 2, QD // 2)]
+    at_b = reserve(4)
+    next_b = [copy(qall.at[0, 2, r, :], prev.at[1, r, :], on_y(1)) for r in parts]
+    own_right_b = [copy(qall.at[0, 2, r, :], qall.at[1, 2, r, :], right, at_b + h) for h, r in enumerate(parts)]
+    prev_right_b = [copy(prev.at[1, r, :], qall.at[1, 2, r, :], right, at_b + h) for h, r in enumerate(parts)]
+    own_left_b = [copy(qall.at[0, 2, r, :], qall.at[3, 2, r, :], left, at_b + 2 + h) for h, r in enumerate(parts)]
+    prev_left_b = [copy(prev.at[1, r, :], qall.at[3, 2, r, :], left, at_b + 2 + h) for h, r in enumerate(parts)]
+
+    def pass_prev_b(h):
+        arrived_if(y > 0, [next_b[h]])
+        if h == 0:
+            arrived_if(y == 0, wrap_in[1])
+        go_if(x == NX - 1, [prev_right_b[h]])
+        go_if(x > 0, [prev_left_b[h]])
+
     relay_r = [copy(qall.at[1, 0], qall.at[2, 0], right, at_relay),
                copy(ids.at[1], ids.at[2], right, at_ids + 2)]
     relay_l = [copy(qall.at[3, 0], qall.at[2, 0], left, at_relay + 1),
                copy(ids.at[3], ids.at[2], left, at_ids + 3)]
     relays = (x == 1) | (x == 2)
 
-    def send_own(n):
-        more = n == 0
-        go_if(x < NX - 1, [own_right[n]] + [own_right_ids] * more)
-        go_if(x == 0, [own_left[n]] + [own_left_ids] * more)
-
-    def send_prev(n):
-        more = n == 0
-        go_if(x == NX - 1, [prev_right[n]] + [prev_right_ids] * more)
-        go_if(x > 0, [prev_left[n]] + [prev_left_ids] * more)
+    def send_own():
+        go_if(x < NX - 1, [own_right, own_right_ids])
+        go_if(x == 0, [own_left, own_left_ids])
+
+    def send_prev():
+        go_if(x == NX - 1, [prev_right, prev_right_ids])
+        go_if(x > 0, [prev_left, prev_left_ids])
 
     class Sum:
         def __init__(self, n):
@@ -345,7 +355,7 @@
         base = mate(d) * (COLS // K * PITCH)
         for k in range(COLS // 128):
             t = dot_nt(rsm[...], qall[s, d, :, k * 128:(k + 1) * 128])
-            t = t[0:128] + (t[128:256] + t[256:384])
+            t = t[0:128] + t[128:256]
             for j in range(2):
                 rows = pl.ds(pl.multiple_of(base + (2 * k + j) * PITCH, 8), K)
                 m[0, rows, :] = t[j * K:(j + 1) * K, 0:128]
@@ -361,23 +371,26 @@
                 at = pl.multiple_of(b * 2 * K + mate(d) * 16, 16)
                 for j, lanes in enumerate((128, 64)):
                     hi, lo = split(m[j, pl.ds(start + b, 16, stride=PITCH), :][:, 0:lanes])
-                    w[s, pl.ds(at, 16), j * 128:j * 128 + lanes] = hi
-                    w[s, pl.ds(at + K, 16), j * 128:j * 128 + lanes] = lo
+                    first = (s // 2) * 256 + j * 128
+                    w[s % 2, pl.ds(at, 16), first:first + lanes] = hi
+                    w[s % 2, pl.ds(at + K, 16), first:first + lanes] = lo
             return carry
 
         lax.fori_loop(0, K, step, 0, unroll=8)
 
-    def scores(s):
+    def scores(pair):
         def step(b, carry):
-            at = pl.multiple_of(b * 128, 128)
-            t = dot_nn(lsm[...], w[s, pl.ds(at, 128), :])
+            t = dot_nn(lsm[...], w[pair, pl.ds(pl.multiple_of(b * 128, 128), 128), :])
             p[pl.ds(pl.multiple_of(b * K, K), K), :] = (t[0:64] + t[64:128]).astype(BF16)
             return carry
 
-        lax.fori_loop(0, K, step, 0, unroll=32)
+        lax.fori_loop(0, K, step, 0, unroll=16)
         value = dot_nn(xbt[...], p[...])
-        same = tcol[:, 0:1] == ids[s, 0:1, 0:QD]
-        st[s] = jnp.where(same, 0.0, value).T
+        for s in (pair, pair + 2):
+            first = (s // 2) * 256
+            same = jnp.concatenate(
+                [tcol[...] == ids[s, 0:1, 0:128], tcol[:, 0:QD - 128] == ids[s, 0:1, 128:QD]], axis=1)
+            st[s] = jnp.where(same, 0.0, value[:, first:first + QD]).T
 
     results = []
 
@@ -393,7 +406,7 @@
     go(regrouped[0, 1])
     go(regrouped[1, 1])
     send_wrap_1()
-    send_next(0)
+    go_if(y < NY - 1, [to_next])
     go_if(y < NY - 1, [to_next_ids])
     go_if(y == NY - 1, [wrap_ids_1])
 
@@ -409,7 +422,7 @@
     sum0 = Sum(0)
     sum0.start()
     sum0.start_x()
-    send_own(0)
+    send_own()
     send_wrap_2()
     go(regrouped[0, 3])
     go(regrouped[1, 2])
@@ -421,58 +434,69 @@
     arrived_if(y == NY - 1, [wrap_ids_1])
     go_if(y == NY - 1, [wrap_ids_2])
     send_wrap_3()
-    wait_prev(0)
+    wait_prev()
     to_next_ids.wait_recv()
-    send_prev(0)
+    send_prev()
     arrived([regrouped[0, 1], regrouped[1, 1]])
     transpose(0, 1)
     transpose(1, 1)
     sum0.start_z()
     go(z_a[0])
-    arrived([regrouped[0, 2], regrouped[0, 3]])
+    def regather(half):
+        lanes = slice(half * HALF, (half + 1) * HALF)
+
+        def step(b, carry):
+            rows = xt[half, pl.ds(b, K, stride=PITCH), :].astype(BF16)
+            xb[pl.ds(pl.multiple_of(b * K, K), K), lanes] = rows
+            return carry
+
+        lax.fori_loop(0, K, step, 0, unroll=8)
+
+    def add_gram(half, total_g):
+        lanes = slice(half * HALF, (half + 1) * HALF)
+
+        def step(k, value):
+            rows = xb[pl.ds(pl.multiple_of(k * 256, 256), 256), lanes]
+            return value + dot_nt(rows, rows)
+
+        return lax.fori_loop(0, 16, step, total_g, unroll=4)
+
+    arrived([regrouped[0, 2]])
     transpose(0, 2)
+    arrived([regrouped[0, 3]])
     transpose(0, 3)
-    arrived([own_right[0], own_left[0], own_right_ids, own_left_ids])
+    regather(0)
+    gram[...] = add_gram(0, jnp.zeros((256, 256), F32))
+    arrived([own_right, own_left, own_right_ids, own_left_ids])
     go_if(relays, relay_r + relay_l)
     go(core_a[1])
     go(core_a[3])
 
-    arrived([regrouped[1, 2], regrouped[1, 3]])
+    arrived([regrouped[1, 2]])
     transpose(1, 2)
+    arrived([regrouped[1, 3]])
     transpose(1, 3)
-
-    def regather(b, carry):
-        for half in range(2):
-            rows = xt[half, pl.ds(b, K, stride=PITCH), :].astype(BF16)
-            xb[pl.ds(pl.multiple_of(b * K, K), K), half * HALF:(half + 1) * HALF] = rows
-        return carry
-
-    lax.fori_loop(0, K, regather, 0, unroll=8)
-
-    def add_gram(k, total_g):
-        rows = xb[pl.ds(pl.multiple_of(k * 256, 256), 256), :]
-        return total_g + dot_nt(rows, rows)
-
-    packed[1] = fold(lax.fori_loop(0, 16, add_gram, jnp.zeros((256, 256), F32), unroll=4))
+    regather(1)
+    packed[1] = fold(add_gram(1, gram[...]))
     sum1 = Sum(1)
     sum1.start()
     sum1.start_x()
     sum0.start_back()
     sum0.finish()
     invert(0)
-    full = inv[0]
-    hi = full.astype(BF16)
-    rest = full - hi.astype(F32)
-    mid, tiny = split(rest)
-    zero = jnp.zeros_like(hi)
-    for n, term in enumerate((hi, mid, tiny)):
+    for n, term in enumerate(split(inv[0])):
+        zero = jnp.zeros_like(term)
         rsm[n * 128:n * 128 + 64, :] = jnp.where(low, term, zero)
         rsm[n * 128 + 64:n * 128 + 128, :] = jnp.where(low, zero, term)
     sum1.start_y()
+    arrived([core_a[1], core_a[3]])
+    prepare(1, (0, 1))
     z_a[0].wait_recv()
-    send_next(1)
-    send_own(1)
+    go_if(y < NY - 1, next_b)
+    go_if(x < NX - 1, own_right_b)
+    go_if(x == 0, own_left_b)
     go(core_b[0])
+    prepare(3, (0, 1))
     eye256 = identity(256)
 
     def put_back(k, carry):
@@ -480,44 +504,41 @@
         xbt[:, pl.ds(at, 256)] = dot_nt(eye256, xb[pl.ds(at, 256), :]).astype(BF16)
         return carry
 
-    lax.fori_loop(0, 16, put_back, 0, unroll=4)
     sum1.start_z()
     arrived_if(x >= 2, relay_r)
     arrived_if(x < 2, relay_l)
     go(z_a[2])
     go(core_a[2])
+    lax.fori_loop(0, 16, put_back, 0, unroll=4)
+    pass_prev_b(0)
     arrived([core_a[0], core_b[0]])
     prepare(0, (0, 1, 2, 3))
-    wait_prev(1)
-    send_prev(1)
+    pass_prev_b(1)
+    core_a[2].wait_recv()
     sum1.start_back()
-    arrived([core_a[1], core_a[3]])
-    prepare(1, (0, 1))
+    prepare(2, (0, 1))
     sum1.finish()
     mean_total = invert(1)
     hi, lo = split(inv[1] * mean_total)
     lsm[0:64, :] = hi
     lsm[64:128, :] = jnp.where(low, lo, jnp.zeros_like(lo))
 
+    z_a[2].wait_recv()
+    go(core_b[2])
+    core_b[2].wait_recv()
+    prepare(2, (2, 3))
+    arrived(own_right_b + own_left_b)
+    go(core_b[1])
+    go(core_b[3])
     scores(0)
     hand_out(0)
-    core_a[2].wait_recv()
-    prepare(2, (0, 1))
-    z_a[2].wait_recv()
-    go(core_b[2])
-    prepare(3, (0, 1))
-    core_b[2].wait_recv()
-    prepare(2, (2, 3))
-    arrived([own_right[1], own_left[1]])
-    go(core_b[1])
-    go(core_b[3])
-    scores(2)
     hand_out(2)
     for s in (1, 3):
         core_b[s].wait_recv()
         prepare(s, (2, 3))
-        scores(s)
-        hand_out(s)
+    scores(1)
+    hand_out(1)
+    hand_out(3)
 
     arrived(results)
     for cond, c in sent:
@@ -550,9 +571,9 @@
         vmem((8, 256), jnp.int32),
         vmem((8, 256), jnp.int32),
         vmem((2, K * PITCH, 128), F32),
-        vmem((STEPS, 2 * K * K, QD), BF16),
+        vmem((2, 2 * K * K, 512), BF16),
         vmem((STEPS, QD, PART), F32),
-        vmem((K * K, QD), BF16),
+        vmem((K * K, 512), BF16),
         vmem((PART, 128), jnp.int32),
         vmem((2, 32, 128), F32),
         vmem((2, 16, 128), F32),
@@ -564,8 +585,9 @@
         vmem((2, 16, 128), F32),
         vmem((2, 32, 128), F32),
         vmem((2, K, 2 * K), F32),
-        vmem((384, 128), BF16),
+        vmem((256, 128), BF16),
         vmem((128, 128), BF16),
+        vmem((256, 256), F32),
         pltpu.SemaphoreType.DMA((N_SEM,)),
         pltpu.SemaphoreType.DMA((N_SEM,)),
     ]

time: 98.2 us -> 94.1 us (0.958)
  Pallas kernels: 95.9 us -> 91.8 us
    pallas_call x1, Pallas kernels: 95.9 us -> 91.8 us  [on_device(): pl.pallas_call(kernel, out_shape=jax.ShapeDtypeStruct((STEPS, QROWS, EX),...]
where the time goes in v4:
time: 94.1 us; the launch traced here: 93.9 us
  Pallas kernels  91.8 us (98%)
  local copies, waits for them, and re-layouts  2.09 us (2%)
    pallas_call x1, Pallas kernels, on_device(): pl.pallas_call(kernel, out_shape=jax.ShapeDtypeStruct((STEPS, QROWS, EX),...  91.8 us
    unnamed x1, local copies, waits for them, and re-layouts  2.09 us

profile of v4, /device:TPU:1, one launch (start us, length us, event | category | flops | bytes accessed | tf_op | source)
XLA Modules:
  0.0 93.9 jit_solution(15334740131077049052)
XLA Ops:
  0.0 91.8 %shard_map.55 = f32[4,48,1024]{2,1,0:T(8,128)} custom-call(bf16[1024,1024]{1,0:T(8,128)(2,1)} %tg.1, bf16[192,1024]{1,0:T(8,128)(2,1)} %qg.1, s32[1,1024]{1,0:T(1,128)} %bitcast.3, s32[1,1024]{1,0:T(1,128)} %bitcast.4, s32[1,192]{1,0:T(1,128)} %bitcast.5), custom_call_target="tpu_custom_call" | custom-call | flops 4000000000 | bytes 8000000 | tf_op jit(solution)/shard_map/pallas_call | solution.py:595
  91.8 2.1 %copy.7 = f32[4,48,1024]{2,1,0:T(8,128)} copy(f32[4,48,1024]{2,1,0:T(8,128)} %shard_map.55) | data formatting | bytes 1572864
